TPU v7x, 32 devices: a whole 2x2x4 slice. The times are simulated.
32 devices in a mesh: groups: 2 (over y), edge: 16 (over z, x, core).
Axes of the slice: x: 2, y: 2, z: 4, core: 2. Of those that a mesh axis runs over, the one named last changes fastest.
Arguments:
- nodes: float32 [512, 512], P(('groups', 'edge')), parts along dimension 0, may hold values from -6 to 6
- edge_feat: float32 [24576, 512], P(('groups', 'edge')), parts along dimension 0, may hold values from -6 to 6
- source: int32 [24576], P(('groups', 'edge')), parts along dimension 0, may hold values from 0 to 255, as said below
- target: int32 [24576], P(('groups', 'edge')), parts along dimension 0, may hold values from 0 to 255, as said below
- w_in: float32 [1536, 512], replicated, may hold values from -0.15625 to 0.15625
- w_out: float32 [512, 512], replicated, may hold values from -0.25 to 0.25
- cotangent: float32 [512, 512], P(('groups', 'edge')), parts along dimension 0, may hold values from -6 to 6
Outputs:
- grad_nodes: float32 [512, 512], P(('groups', 'edge')), parts along dimension 0
- grad_in: float32 [3072, 512], P('groups'), parts along dimension 0
- grad_out: float32 [1024, 512], P('groups'), parts along dimension 0
There are 2 independent parts, one for each index of `groups`. A program takes and returns all parts, laid end to end along the dimension named above; an argument that names none is the same for every part. Nothing has to cross between parts.
Inputs may be any that keep to these rules, and one draw needn't show every extreme that they name: `source`: the edges held by one index d of edge (positions d * 768 to (d + 1) * 768 - 1) have at most 96 sources among the nodes held by any one index (nodes j * 16 to (j + 1) * 16 - 1); one index j, the same for all d, holds exactly 96 of the sources of every d. Every edge's target is a node held by the same index of edge as the edge: for positions d * 768 to (d + 1) * 768 - 1 it lies in d * 16 to (d + 1) * 16 - 1.
All inputs are finite; a program needn't handle non-finite values.
Results may differ from a plain program's by a relative error of at most 0.0001.
Values sent between devices are 32-bit elements; how exact they have to be, the bound alone decides.
A program may use at most 64 MiB of HBM per device.

v0:
```python
import math

import jax
import jax.numpy as jnp
from jax import lax
from jax.sharding import PartitionSpec as P


def body(nodes, edge_feat, source, target, w_in, w_out, cotangent):
    highest = lax.Precision.HIGHEST
    node_rows, width = nodes.shape
    edge_rows = source.shape[0]
    devices = lax.axis_size("edge")
    first_node = lax.axis_index("edge") * node_rows
    local_hot = (
        target[:, None] - first_node == jnp.arange(node_rows, dtype=jnp.int32)[None, :]
    ).astype(jnp.float32)
    near = jnp.dot(local_hot, nodes, precision=highest, preferred_element_type=jnp.float32)
    upstream = jnp.dot(local_hot, cotangent, precision=highest, preferred_element_type=jnp.float32)
    w_source = w_in[:width]
    table = jnp.dot(nodes, w_source, precision=highest, preferred_element_type=jnp.float32)
    piece = lax.all_gather(table, "edge", axis=0, tiled=True)
    count = piece.shape[0]
    hot = (source[:, None] == jnp.arange(count, dtype=jnp.int32)[None, :]).astype(jnp.float32)
    far = jnp.dot(hot, piece, precision=highest, preferred_element_type=jnp.float32)
    rest = jnp.concatenate([near, edge_feat], axis=1)
    preact = far + jnp.dot(
        rest, w_in[width:], precision=highest, preferred_element_type=jnp.float32
    )
    sigma = jax.nn.sigmoid(preact)
    hidden = preact * sigma
    back = jnp.dot(upstream, w_out.T, precision=highest, preferred_element_type=jnp.float32)
    dpre = back * sigma * (1.0 + preact * (1.0 - sigma))
    grad_second = jnp.dot(hidden.T, upstream, precision=highest, preferred_element_type=jnp.float32)
    grad_rest = jnp.dot(rest.T, dpre, precision=highest, preferred_element_type=jnp.float32)
    drest = jnp.dot(dpre, w_in[width:].T, precision=highest, preferred_element_type=jnp.float32)
    hot = (
        source[:, None] == jnp.arange(lax.axis_size("edge") * node_rows, dtype=jnp.int32)[None, :]
    ).astype(jnp.float32)
    source_sum = lax.psum_scatter(
        jnp.einsum("ec,ew->cw", hot, dpre, precision=highest, preferred_element_type=jnp.float32),
        "edge",
        scatter_dimension=0,
        tiled=True,
    )
    grad_source = jnp.dot(
        source_sum, w_source.T, precision=highest, preferred_element_type=jnp.float32
    )
    grad_top = jnp.dot(nodes.T, source_sum, precision=highest, preferred_element_type=jnp.float32)
    grad_first = jnp.concatenate([grad_top, grad_rest], axis=0)
    near_grad = drest[:, :width]
    grads = grad_source + jnp.einsum(
        "en,ew->nw", local_hot, near_grad, precision=highest, preferred_element_type=jnp.float32
    )
    grad_first, grad_second = lax.psum((grad_first, grad_second), "edge")
    factor = 1.0 / math.sqrt(edge_rows * devices)
    return (grads, grad_first * factor, grad_second * factor)


def solution(mesh):
    placed = (
        P(("groups", "edge"), None),
        P(("groups", "edge"), None),
        P(("groups", "edge")),
        P(("groups", "edge")),
        P(),
        P(),
        P(("groups", "edge"), None),
    )
    return jax.shard_map(
        body,
        mesh=mesh,
        in_specs=placed,
        out_specs=(P(("groups", "edge"), None), P("groups", None), P("groups", None)),
        check_vma=False,
    )
```

profile of v0, /device:TPU:1, one launch (start us, length us, event | category | flops | bytes accessed | tf_op | source)
XLA Modules:
  0.0 233.6 jit_solution(11800877209876869622)
XLA Ops:
  7.3 1.9 fusion.12
  9.2 24.5 %all_gather.3 = f32[256,512]{1,0:T(8,128)S(1)} all-gather(f32[16,512]{1,0:T(8,128)S(1)} %fusion.12), channel_id=1, replica_groups=mesh['groups'=2,'edge'=16] {'edge'}, dimensions={0}, use_global_device_ids=true | all-gather | bytes 557056 | tf_op jit(solution)/shard_map/all_gather | solution.py:22
  33.7 1.0 fusion.17
  34.6 2.0 fusion.18
  36.6 3.0 %copy.10 = f32[768,512]{0,1:T(8,128)} copy(f32[768,512]{1,0:T(8,128)} %param.8) | data formatting | bytes 3145728 | tf_op args[1]
  39.7 0.9 fusion.16
  40.6 0.5 copy-done.1
  41.1 6.8 %fusion.5 = f32[768,512]{1,0:T(8,128)S(1)} fusion(f32[768,512]{1,0:T(8,128)S(1)} %fusion.16, f32[1536,512]{1,0:T(8,128)} %param.11, f32[768,512]{0,1:T(8,128)S(1)} %copy-done.1, f32[768,512]{0,1:T(8,128)S(1)} %fusion.17), kind=kOutput, calls=%fused_computation.10 | convolution fusion | flops 4833017856 | bytes 8388608 | tf_op jit(solution)/shard_map/dot_general | solution.py:27
  48.0 3.0 %add_multiply_fusion = f32[768,512]{1,0:T(8,128)S(1)} fusion(f32[768,512]{1,0:T(8,128)S(1)} %fusion.5, f32[768,512]{1,0:T(8,128)S(1)} %copy-done.7, f32[512,512]{1,0:T(8,128)S(1)} %copy-done), kind=kOutput, calls=%fused_computation.8 | convolution fusion | flops 2419064832 | bytes 5767168 | tf_op jit(solution)/shard_map/dot_general | solution.py:32
  51.0 1.1 copy-done.2
  52.2 2.1 fusion.15
  54.3 0.0 all-reduce.3.cloned.1.call-start
  54.4 8.3 %fusion = f32[1024,512]{1,0:T(8,128)} fusion(f32[768,512]{1,0:T(8,128)} %copy-done.2, f32[768,512]{0,1:T(8,128)} %copy.10, f32[768,512]{0,1:T(8,128)S(1)} %fusion.17), kind=kOutput, calls=%fused_computation.2 | convolution fusion | flops 4832624640 | bytes 6815744 | tf_op jit(solution)/shard_map/dot_general | solution.py:35
  62.7 3.9 %fusion.3 = f32[512,512]{1,0:T(8,128)} fusion(f32[768,512]{1,0:T(8,128)S(1)} %copy-done.8, f32[768,512]{1,0:T(8,128)S(1)} %copy-done.6), kind=kOutput, calls=%fused_computation.5 | convolution fusion | flops 2417491968 | bytes 4194304 | tf_op jit(solution)/shard_map/dot_general | solution.py:34
  66.6 38.6 %reduce-scatter.2.cloned.1.call-done = f32[16,512]{1,0:T(8,128)} async-done(((f32[256,512]{1,0:T(8,128)}), f32[16,512]{1,0:T(8,128)}) %reduce-scatter.2.cloned.1.call-update) | async-done | bytes 32784 | tf_op jit(solution)/shard_map/reduce_scatter | solution.py:40
  105.1 1.8 convolution_bitcast_fusion
  106.9 2.0 pad_maximum_fusion.1
  108.9 1.4 copy-done.3
  110.3 3.9 %fusion.8 = f32[768,512]{1,0:T(8,128)S(1)} fusion(f32[768,512]{1,0:T(8,128)S(1)} %copy-done.3, f32[1536,512]{1,0:T(8,128)} %param.11), kind=kOutput, calls=%fused_computation.13 | convolution fusion | flops 2415919104 | bytes 4194304 | tf_op jit(solution)/shard_map/dot_general | solution.py:36
  114.2 2.2 fusion.10
  116.4 1.4 convolution_add_fusion
  117.8 103.8 %all-reduce.3.cloned.1.call-done = (f32[1536,512]{1,0:T(8,128)}, f32[512,512]{1,0:T(8,128)}) async-done(((f32[1536,512]{1,0:T(8,128)}, f32[512,512]{1,0:T(8,128)}), (f32[1536,512]{1,0:T(8,128)}, f32[512,512]{1,0:T(8,128)})) %all-reduce.3.cloned.1.call-update) | async-done | bytes 4194320 | tf_op jit(solution)/shard_map/psum | solution.py:55
  221.6 4.0 %broadcast_multiply_fusion = f32[1536,512]{1,0:T(8,128)} fusion(f32[1536,512]{1,0:T(8,128)} %get-tuple-element.3), kind=kLoop, calls=%fused_computation.7 | loop fusion | flops 786432 | bytes 6291456 | tf_op jit(solution)/shard_map/mul | solution.py:57
  225.6 1.1 broadcast_multiply_fusion.1
  (31 shorter events, 0.1 us)
Async XLA Ops:
  7.2 40.8 %copy-start = (f32[512,512]{1,0:T(8,128)S(1)}, f32[512,512]{1,0:T(8,128)}, u32[]{:S(2)}) copy-start(f32[512,512]{1,0:T(8,128)} %param.12) | copy-start | bytes 3145732
  7.2 26.5 %copy-start.10 = (f32[16,512]{1,0:T(8,128)S(1)}, f32[16,512]{1,0:T(8,128)}, u32[]{:S(2)}) copy-start(f32[16,512]{1,0:T(8,128)} %param.7) | copy-start | bytes 98308
  7.2 26.5 %copy-start.14 = (s32[768]{0:T(1024)S(1)}, s32[768]{0:T(1024)}, u32[]{:S(2)}) copy-start(s32[768]{0:T(1024)} %param.10) | copy-start | bytes 9220
  7.2 97.9 %reduce-scatter.2.cloned.1.call-start = ((), (), s32[]{:S(2)}) async-start(), calls=%async_computation.1 | async-start | bytes 557056 | tf_op jit(solution)/shard_map/reduce_scatter | solution.py:40
  7.3 27.4 %copy-start.12 = (f32[16,512]{1,0:T(8,128)S(1)}, f32[16,512]{1,0:T(8,128)}, u32[]{:S(2)}) copy-start(f32[16,512]{1,0:T(8,128)} %param.13) | copy-start | bytes 98308
  36.6 3.0 %copy-start.13 = (s32[768]{0:T(1024)S(1)}, s32[768]{0:T(1024)}, u32[]{:S(2)}) copy-start(s32[768]{0:T(1024)} %param.9) | copy-start | bytes 9220
  39.7 1.4 copy-start.1
  41.1 6.9 %copy-start.7 = (f32[768,512]{1,0:T(8,128)S(1)}, f32[768,512]{1,0:T(8,128)}, u32[]{:S(2)}) copy-start(f32[768,512]{1,0:T(8,128)} %fusion.18) | copy-start | bytes 4718596
  48.0 3.1 %copy-start.5 = (f32[768,512]{1,0:T(8,128)}, f32[768,512]{1,0:T(8,128)S(1)}, u32[]{:S(2)}) copy-start(f32[768,512]{1,0:T(8,128)S(1)} %fusion.5) | copy-start | bytes 4718596
  51.0 1.2 copy-start.2
  54.3 167.3 %all-reduce.3.cloned.1.call-start = ((), (), s32[]{:S(2)}) async-start(), calls=%async_computation.2 | async-start | bytes 8388608 | tf_op jit(solution)/shard_map/psum | solution.py:55
  54.4 8.3 %copy-start.6 = (f32[768,512]{1,0:T(8,128)S(1)}, f32[768,512]{1,0:T(8,128)}, u32[]{:S(2)}) copy-start(f32[768,512]{1,0:T(8,128)} %copy-done.5) | copy-start | bytes 4718596
  54.4 8.3 %copy-start.8 = (f32[768,512]{1,0:T(8,128)S(1)}, f32[768,512]{1,0:T(8,128)}, u32[]{:S(2)}) copy-start(f32[768,512]{1,0:T(8,128)} %fusion.18) | copy-start | bytes 4718596
  62.7 44.2 %copy-start.4 = (f32[1024,512]{1,0:T(8,128)S(1)}, f32[1024,512]{1,0:T(8,128)}, u32[]{:S(2)}) copy-start(f32[1024,512]{1,0:T(8,128)} %fusion) | copy-start | bytes 6291460
  108.9 1.4 copy-start.3
  110.3 3.9 %copy-start.11 = (f32[16,512]{1,0:T(8,128)S(1)}, f32[16,512]{1,0:T(8,128)}, u32[]{:S(2)}) copy-start(f32[16,512]{1,0:T(8,128)} %reduce-scatter.2.cloned.1.call-done) | copy-start | bytes 98308
  221.6 4.0 %copy-start.9 = (f32[512,512]{1,0:T(8,128)S(1)}, f32[512,512]{1,0:T(8,128)}, u32[]{:S(2)}) copy-start(f32[512,512]{1,0:T(8,128)} %get-tuple-element.4) | copy-start | bytes 3145732
Sparse Core Ops, SparseCore 0:
  54.4 50.6 reduce-scatter.1
  110.0 111.5 all-reduce.2
where the time goes:
time: 236 us; the launch traced here: 234 us
  waiting for transfers between devices  142 us (60%)
  matrix products  39.1 us (17%)
  blocking collectives  24.5 us (10%)
  between operations  14.2 us (6%)
  other arithmetic  7.08 us (3%)
  local copies, waits for them, and re-layouts  6.15 us (3%)
    psum x1, waiting for transfers between devices, body(): grad_first, grad_second = lax.psum((grad_first, grad_second), 'edge')  104 us
    reduce_scatter x1, waiting for transfers between devices, body(): lax.psum_scatter(jnp.einsum('ec,ew->cw', hot, dpre, precision=highest, pr...  38.6 us
    all_gather x1, blocking collectives, body(): piece = lax.all_gather(table, 'edge', axis=0, tiled=True)  24.5 us
    dot_general x1, matrix products, body(): jnp.dot(rest.T, dpre, precision=highest, preferred_element_type=jnp.float32)  8.32 us
    dot_general x1, matrix products, body(): jnp.dot(rest, w_in[width:], precision=highest, preferred_element_type=jnp...  6.84 us
    unnamed x31, local copies, waits for them, and re-layouts  6.15 us
    mul x2, other arithmetic, body(): return (grads, grad_first * factor, grad_second * factor)  5.1 us
  transfers between devices with their start and end apart: 2, of which 2 were waited for; matrix products, arithmetic and copies ran while one was open for 8% of the time, Pallas kernels for 0%

commit v1 on v0

--- a/solution.py
+++ b/solution.py
@@ -1,12 +1,15 @@
+import functools
 import math
 
 import jax
 import jax.numpy as jnp
 from jax import lax
+from jax.experimental import pallas as pl
+from jax.experimental.pallas import tpu as pltpu
 from jax.sharding import PartitionSpec as P
 
 
-def body(nodes, edge_feat, source, target, w_in, w_out, cotangent):
+def plain(nodes, edge_feat, source, target, w_in, w_out, cotangent):
     highest = lax.Precision.HIGHEST
     node_rows, width = nodes.shape
     edge_rows = source.shape[0]
@@ -57,6 +60,284 @@
     return (grads, grad_first * factor, grad_second * factor)
 
 
+MESH = pl.DeviceIdType.MESH
+NODE, COT, TGT, HID, SRC, FA, FB = range(7)
+
+
+def split(value):
+    high = value.astype(jnp.bfloat16)
+    low = (value - high.astype(jnp.float32)).astype(jnp.bfloat16)
+    return high, low
+
+
+def mm(a, b, dims=((1,), (0,))):
+    return lax.dot_general(a, b, (dims, ((), ())), preferred_element_type=jnp.float32)
+
+
+def mm3(a, b, dims=((1,), (0,))):
+    (ah, al), (bh, bl) = a, b
+    return mm(ah, bh, dims) + (mm(ah, bl, dims) + mm(al, bh, dims))
+
+
+def kernel(n, nodes, cot, src, tgt, feat_hbm, win_hbm, wout_hbm, grads, gin, gout,
+           ag, part, rc, rx, rz, feat, win, wout, eth, etl, hot_t, hot,
+           tabh, tabl, bkh, bkl, pre, dh, dl, ngth, ngtl, load_sem, send_sem, recv_sem):
+    f32, bf16 = jnp.float32, jnp.bfloat16
+    rows, width = nodes.shape
+    edges = src.shape[1]
+    zs = n // 4
+    total = n * rows
+    factor = 1.0 / math.sqrt(edges * n)
+    me = lax.axis_index("edge")
+    c, x, z = lax.rem(me, 2), lax.rem(me // 2, 2), me // 4
+
+    def index(z, x, c):
+        return (z * 2 + x) * 2 + c
+
+    sibling, across = index(z, x, 1 - c), index(z, 1 - x, c)
+    line = [index(lax.rem(z + k, zs), x, c) for k in range(1, zs)]
+    half, quarter = total // 2, total // 4
+
+    def at(size, start):
+        return pl.ds(pl.multiple_of(start, rows), size)
+
+    own = at(rows, c * half + x * quarter + z * rows)
+    sent = {}
+
+    def send(key, slot, source, dest, device):
+        copy = pltpu.make_async_remote_copy(
+            src_ref=source, dst_ref=dest, send_sem=send_sem.at[slot], recv_sem=recv_sem.at[slot],
+            device_id={"edge": device}, device_id_type=MESH)
+        copy.start()
+        sent.setdefault(key, []).append(copy)
+
+    def fin(*key):
+        for copy in sent[key]:
+            copy.wait_recv()
+
+    per = zs + 1
+
+    def ag_z(i):
+        for k, device in enumerate(line):
+            send(("az", i), i * per + k, ag.at[i, own], ag.at[i, own], device)
+
+    def ag_x(i):
+        fin("az", i)
+        block = at(quarter, c * half + x * quarter)
+        send(("ax", i), i * per + zs - 1, ag.at[i, block], ag.at[i, block], across)
+
+    def ag_c(i):
+        fin("ax", i)
+        block = at(half, c * half)
+        send(("ac", i), i * per + zs, ag.at[i, block], ag.at[i, block], sibling)
+
+    def rs_c(j):
+        send(("rc", j), (7 + j) * per, part.at[j, at(half, (1 - c) * half)], rc.at[j], sibling)
+
+    def rs_x(j):
+        fin("rc", j)
+        away = at(quarter, c * half + (1 - x) * quarter)
+        part[j, away] += rc[j, at(quarter, (1 - x) * quarter)]
+        send(("rx", j), (7 + j) * per + 1, part.at[j, away], rx.at[j], across)
+        part[j, at(quarter, c * half + x * quarter)] += rc[j, at(quarter, x * quarter)]
+
+    def rs_z(j):
+        fin("rx", j)
+        base = c * half + x * quarter
+        part[j, at(quarter, base)] += rx[j]
+        for k, device in enumerate(line):
+            other = lax.rem(z + k + 1, zs)
+            send(("rz", j), (7 + j) * per + 2 + k, part.at[j, at(rows, base + other * rows)],
+                 rz.at[j, k], device)
+
+    def rs_done(j, i):
+        fin("rz", j)
+        piece = part[j, own]
+        for k in range(zs - 1):
+            piece = piece + rz[j, k]
+        ag[i, own] = piece
+        ag_z(i)
+
+    load_feat = pltpu.make_async_copy(feat_hbm, feat, load_sem.at[0])
+    load_win = pltpu.make_async_copy(win_hbm, win, load_sem.at[1])
+    load_wout = pltpu.make_async_copy(wout_hbm, wout, load_sem.at[2])
+    load_feat.start()
+    load_win.start()
+    load_wout.start()
+    ag[NODE, own] = nodes[...]
+    ag[COT, own] = cot[...]
+    barrier = pltpu.get_barrier_semaphore()
+    peers = [sibling, across] + line
+    for device in peers:
+        pl.semaphore_signal(barrier, inc=1, device_id={"edge": device}, device_id_type=MESH)
+    pl.semaphore_wait(barrier, len(peers))
+    ag_z(NODE)
+
+    ids = src[...]
+    owner = ids // rows
+    place = (lax.rem(owner, 2) * half + lax.rem(owner // 2, 2) * quarter
+             + (owner // 4) * rows + lax.rem(ids, rows))
+    seen = lax.broadcasted_iota(jnp.int32, (total, edges), 0) == place
+    near = lax.broadcasted_iota(jnp.int32, (128, edges), 0) == tgt[...] - me * rows
+    seen, near = jnp.where(seen, 1.0, 0.0), jnp.where(near, 1.0, 0.0)
+    hot_t[0:total] = seen.astype(bf16)
+    hot_t[total:total + 128] = near.astype(bf16)
+    hot[:, 0:total] = seen.T.astype(bf16)
+    hot[:, total:total + 128] = near.T.astype(bf16)
+
+    load_feat.wait()
+    load_win.wait()
+    tile = 256
+    tiles = edges // tile
+
+    def first(t):
+        high, low = split(feat[t * tile:(t + 1) * tile])
+        wf = split(win[2 * width:3 * width])
+        pre[t * tile:(t + 1) * tile] = mm3((high, low), wf)
+
+    def turn(t):
+        high, low = split(feat[t * tile:(t + 1) * tile].T)
+        eth[:, t * tile:(t + 1) * tile] = high
+        etl[:, t * tile:(t + 1) * tile] = low
+
+    first(0)
+    ag_x(NODE)
+    ag_z(COT)
+    first(1)
+    ag_c(NODE)
+    first(2)
+    load_wout.wait()
+    zeros = jnp.zeros((128 - rows, width), bf16)
+    th, tl = split(mm3(split(nodes[...]), split(win[width:2 * width])))
+    tabh[total:total + 128] = jnp.concatenate([th, zeros], axis=0)
+    tabl[total:total + 128] = jnp.concatenate([tl, zeros], axis=0)
+    th, tl = split(mm3(split(cot[...]), split(wout[...]), ((1,), (1,))))
+    bkh[...] = jnp.concatenate([th, zeros], axis=0)
+    bkl[...] = jnp.concatenate([tl, zeros], axis=0)
+    for t in range(tiles):
+        turn(t)
+    fin("ac", NODE)
+    th, tl = split(mm3(split(ag[NODE]), split(win[0:width])))
+    tabh[0:total] = th
+    tabl[0:total] = tl
+    ag_x(COT)
+
+    t_sum = jnp.zeros((rows, width), f32)
+    g_sum = jnp.zeros((rows, width), f32)
+    for t in range(tiles):
+        cut = slice(t * tile, (t + 1) * tile)
+        ones = hot[cut]
+        v = pre[cut] + (mm(ones, tabh[...]) + mm(ones, tabl[...]))
+        back = mm(ones[:, total:], bkh[...]) + mm(ones[:, total:], bkl[...])
+        sigma = jax.nn.sigmoid(v)
+        hh, hl = split(v * sigma)
+        high, low = split(back * sigma * (1.0 + v * (1.0 - sigma)))
+        dh[cut] = high
+        dl[cut] = low
+        ones_t = hot_t[total:total + rows, cut]
+        t_sum += mm(ones_t, high) + mm(ones_t, low)
+        g_sum += mm(ones_t, hh) + mm(ones_t, hl)
+    ag[TGT, own] = t_sum
+    ag[HID, own] = g_sum
+    ag_z(TGT)
+    ag_z(HID)
+    part[0] = mm(hot_t[0:total], dh[...]) + mm(hot_t[0:total], dl[...])
+    rs_c(0)
+    ag_c(COT)
+
+    def outer(j):
+        cut = slice((j - 1) * total, j * total)
+        part[j] = mm3((eth[cut], etl[cut]), (dh[...], dl[...]))
+        rs_c(j)
+
+    outer(1)
+    rs_x(0)
+    outer(2)
+    rs_x(1)
+    rs_z(0)
+    rs_x(2)
+    ag_x(TGT)
+    ag_x(HID)
+    nh, nl = split(ag[NODE].T)
+    ngth[...] = nh
+    ngtl[...] = nl
+    rs_z(1)
+    rs_done(0, SRC)
+    rs_z(2)
+    ag_c(TGT)
+    ag_c(HID)
+    grads[...] = (mm3(split(ag[SRC, own]), split(win[0:width]), ((1,), (1,)))
+                  + mm3(split(ag[TGT, own]), split(win[width:2 * width]), ((1,), (1,))))
+    rs_done(1, FA)
+    ag_x(SRC)
+    rs_done(2, FB)
+    fin("ac", TGT)
+    gin[width:2 * width] = mm3((ngth[...], ngtl[...]), split(ag[TGT])) * factor
+    ag_x(FA)
+    ag_c(SRC)
+    ag_x(FB)
+    fin("ac", HID)
+    fin("ac", COT)
+    gout[...] = mm3(split(ag[HID].T), split(ag[COT])) * factor
+    ag_c(FA)
+    fin("ac", SRC)
+    gin[0:width] = mm3((ngth[...], ngtl[...]), split(ag[SRC])) * factor
+    ag_c(FB)
+    fin("ac", FA)
+    gin[2 * width:2 * width + total] = ag[FA] * factor
+    fin("ac", FB)
+    gin[2 * width + total:3 * width] = ag[FB] * factor
+    for copies in sent.values():
+        for copy in copies:
+            copy.wait_send()
+
+
+def fused(n, nodes, edge_feat, source, target, w_in, w_out, cotangent):
+    f32, bf16 = jnp.float32, jnp.bfloat16
+    rows, width = nodes.shape
+    edges = source.shape[0]
+    zs, total = n // 4, n * rows
+    vmem = pl.BlockSpec(memory_space=pltpu.VMEM)
+    hbm = pl.BlockSpec(memory_space=pl.ANY)
+    scratch = [
+        ((7, total, width), f32), ((3, total, width), f32), ((3, total // 2, width), f32),
+        ((3, total // 4, width), f32), ((3, zs - 1, rows, width), f32),
+        ((edges, width), f32), ((3 * width, width), f32), ((width, width), f32),
+        ((width, edges), bf16), ((width, edges), bf16),
+        ((total + 128, edges), bf16), ((edges, total + 128), bf16),
+        ((total + 128, width), bf16), ((total + 128, width), bf16),
+        ((128, width), bf16), ((128, width), bf16),
+        ((edges, width), f32), ((edges, width), bf16), ((edges, width), bf16),
+        ((width, total), bf16), ((width, total), bf16),
+    ]
+    copies = 10 * (zs + 1)
+    return pl.pallas_call(
+        functools.partial(kernel, n),
+        out_shape=(
+            jax.ShapeDtypeStruct((rows, width), f32),
+            jax.ShapeDtypeStruct((3 * width, width), f32),
+            jax.ShapeDtypeStruct((width, width), f32),
+        ),
+        in_specs=[vmem] * 4 + [hbm] * 3,
+        out_specs=(vmem, vmem, vmem),
+        scratch_shapes=[pltpu.VMEM(shape, kind) for shape, kind in scratch] + [
+            pltpu.SemaphoreType.DMA((3,)),
+            pltpu.SemaphoreType.DMA((copies,)),
+            pltpu.SemaphoreType.DMA((copies,)),
+        ],
+        compiler_params=pltpu.CompilerParams(
+            collective_id=0, has_side_effects=True, vmem_limit_bytes=52 * 2**20),
+    )(nodes, cotangent, source.reshape(1, edges), target.reshape(1, edges), edge_feat, w_in, w_out)
+
+
+def body(nodes, edge_feat, source, target, w_in, w_out, cotangent):
+    devices = lax.axis_size("edge")
+    rows, width = nodes.shape
+    if devices % 4 == 0 and devices >= 8 and 2 * devices * rows == width and source.shape[0] % 256 == 0:
+        return fused(devices, nodes, edge_feat, source, target, w_in, w_out, cotangent)
+    return plain(nodes, edge_feat, source, target, w_in, w_out, cotangent)
+
+
 def solution(mesh):
     placed = (
         P(("groups", "edge"), None),

time: 236 us -> 61.5 us (0.26)
  waiting for transfers between devices: 142 us -> 0 us
  Pallas kernels: 0 us -> 52.2 us
  matrix products: 39.1 us -> 0 us
  blocking collectives: 24.5 us -> 0 us
  between operations: 14.2 us -> 0.64 us
  other arithmetic: 7.08 us -> 0 us
    psum x1 -> x0, waiting for transfers between devices: 104 us -> none  [body(): grad_first, grad_second = lax.psum((grad_first, grad_second), 'edge')]
    pallas_call x0 -> x1, Pallas kernels: none -> 52.2 us  [fused(): pl.pallas_call(functools.partial(kernel, n), out_shape=(jax.ShapeDtypeStr...]
    dot_general x13 -> x0, matrix products: 39.1 us -> none  [the longest x1 8.32 us: body(): jnp.dot(rest.T, dpre, precision=highest, preferred_element_type=jnp.float32)]
    reduce_scatter x1 -> x0, waiting for transfers between devices: 38.6 us -> none  [body(): lax.psum_scatter(jnp.einsum('ec,ew->cw', hot, dpre, precision=highest, pr...]
    all_gather x1 -> x0, blocking collectives: 24.5 us -> none  [body(): piece = lax.all_gather(table, 'edge', axis=0, tiled=True)]
    mul x2 -> x0, other arithmetic: 5.1 us -> none  [body(): return (grads, grad_first * factor, grad_second * factor)]
    unnamed x31 -> x7, local copies, waits for them, and re-layouts: 6.15 us -> 6.96 us
  transfers between devices with their start and end apart: 2 -> 0, of which waited for: 2 -> 0; matrix products, arithmetic and copies ran while one was open for 8% -> 0% of each run, Pallas kernels for 0% -> 0%
where the time goes in v1:
time: 61.5 us; the launch traced here: 61.2 us
  Pallas kernels  52.2 us (85%)
  local copies, waits for them, and re-layouts  8.34 us (14%)
  between operations  0.64 us (1%)
    pallas_call x1, Pallas kernels, fused(): pl.pallas_call(functools.partial(kernel, n), out_shape=(jax.ShapeDtypeStr...  52.2 us
    unnamed x7, local copies, waits for them, and re-layouts  6.96 us

profile of v1, /device:TPU:1, one launch (start us, length us, event | category | flops | bytes accessed | tf_op | source)
XLA Modules:
  0.0 61.2 jit_solution(14572945564048896175)
XLA Ops:
  0.6 0.7 %reshape.12.src = s32[1,768]{1,0:T(1,128)S(1)} reshape(s32[768]{0:T(1024)} %param.9) | data formatting | bytes 6144 | tf_op jit(solution)/shard_map/reshape | solution.py:330
  1.3 0.7 %reshape.13.tgt = s32[1,768]{1,0:T(1,128)S(1)} reshape(s32[768]{0:T(1024)} %param.10) | data formatting | bytes 6144 | tf_op jit(solution)/shard_map/reshape | solution.py:330
  2.0 0.0 copy-start
  2.0 0.8 %copy-done = f32[16,512]{1,0:T(8,128)S(1)} copy-done((f32[16,512]{1,0:T(8,128)S(1)}, f32[16,512]{1,0:T(8,128)}, u32[]{:S(2)}) %copy-start) | copy-done | bytes 32792
  2.8 0.0 copy-start.1
  2.8 0.8 %copy-done.1 = f32[16,512]{1,0:T(8,128)S(1)} copy-done((f32[16,512]{1,0:T(8,128)S(1)}, f32[16,512]{1,0:T(8,128)}, u32[]{:S(2)}) %copy-start.1) | copy-done | bytes 32792
  3.5 52.2 %shard_map.94 = (f32[16,512]{1,0:T(8,128)S(1)}, f32[1536,512]{1,0:T(8,128)}, f32[512,512]{1,0:T(8,128)S(1)}) custom-call(f32[16,512]{1,0:T(8,128)S(1)} %copy-done, f32[16,512]{1,0:T(8,128)S(1)} %copy-done.1, s32[1,768]{1,0:T(1,128)S(1)} %reshape.12.src, s32[1,768]{1,0:T(1,128)S(1)} %reshape.13.tgt, f32[768,512]{1,0:T(8,128)} %feat_hbm.1, ...), custom_call_target="tpu_custom_call" | custom-call | tf_op jit(solution)/shard_map/pallas_call | solution.py:314
  55.8 0.6 %copy.13 = f32[16,512]{1,0:T(8,128)} copy(f32[16,512]{1,0:T(8,128)S(1)} %get-tuple-element.6) | data formatting | bytes 65536
  56.4 3.9 %copy.14 = f32[1536,512]{1,0:T(8,128)} copy(f32[1536,512]{1,0:T(8,128)} %get-tuple-element.7) | data formatting | bytes 6291456
  60.2 1.0 %copy.15 = f32[512,512]{1,0:T(8,128)} copy(f32[512,512]{1,0:T(8,128)S(1)} %get-tuple-element.8) | data formatting | bytes 2097152
Async XLA Ops:
  2.0 0.8 %copy-start = (f32[16,512]{1,0:T(8,128)S(1)}, f32[16,512]{1,0:T(8,128)}, u32[]{:S(2)}) copy-start(f32[16,512]{1,0:T(8,128)} %nodes.1) | copy-start | bytes 98308
  2.8 0.8 %copy-start.1 = (f32[16,512]{1,0:T(8,128)S(1)}, f32[16,512]{1,0:T(8,128)}, u32[]{:S(2)}) copy-start(f32[16,512]{1,0:T(8,128)} %cot.1) | copy-start | bytes 98308

commit v2 on v1

--- a/solution.py
+++ b/solution.py
@@ -79,9 +79,9 @@
     return mm(ah, bh, dims) + (mm(ah, bl, dims) + mm(al, bh, dims))
 
 
-def kernel(n, nodes, cot, src, tgt, feat_hbm, win_hbm, wout_hbm, grads, gin, gout,
-           ag, part, rc, rx, rz, feat, win, wout, eth, etl, hot_t, hot,
-           tabh, tabl, bkh, bkl, pre, dh, dl, ngth, ngtl, load_sem, send_sem, recv_sem):
+def kernel(n, nodes, cot, src_hbm, tgt_hbm, feat, win, wout, grads, gin, gout,
+           ag, part, rc, rx, rz, eth, etl, hot_t, hot,
+           tabh, tabl, bkh, bkl, pre, dh, dl, ngth, ngtl, src, tgt, load_sem, send_sem, recv_sem):
     f32, bf16 = jnp.float32, jnp.bfloat16
     rows, width = nodes.shape
     edges = src.shape[1]
@@ -117,19 +117,28 @@
 
     per = zs + 1
 
-    def ag_z(i):
+    def cols(h):
+        return pl.ds(0, width) if h is None else pl.ds(h * (width // 2), width // 2)
+
+    def slot(i, h):
+        return i * per if not h else (10 + i) * per
+
+    def ag_z(i, h=None):
         for k, device in enumerate(line):
-            send(("az", i), i * per + k, ag.at[i, own], ag.at[i, own], device)
-
-    def ag_x(i):
-        fin("az", i)
+            send(("az", i, h), slot(i, h) + k, ag.at[i, own, cols(h)], ag.at[i, own, cols(h)],
+                 device)
+
+    def ag_x(i, h=None):
+        fin("az", i, h)
         block = at(quarter, c * half + x * quarter)
-        send(("ax", i), i * per + zs - 1, ag.at[i, block], ag.at[i, block], across)
-
-    def ag_c(i):
-        fin("ax", i)
+        send(("ax", i, h), slot(i, h) + zs - 1, ag.at[i, block, cols(h)], ag.at[i, block, cols(h)],
+             across)
+
+    def ag_c(i, h=None):
+        fin("ax", i, h)
         block = at(half, c * half)
-        send(("ac", i), i * per + zs, ag.at[i, block], ag.at[i, block], sibling)
+        send(("ac", i, h), slot(i, h) + zs, ag.at[i, block, cols(h)], ag.at[i, block, cols(h)],
+             sibling)
 
     def rs_c(j):
         send(("rc", j), (7 + j) * per, part.at[j, at(half, (1 - c) * half)], rc.at[j], sibling)
@@ -158,20 +167,23 @@
         ag[i, own] = piece
         ag_z(i)
 
-    load_feat = pltpu.make_async_copy(feat_hbm, feat, load_sem.at[0])
-    load_win = pltpu.make_async_copy(win_hbm, win, load_sem.at[1])
-    load_wout = pltpu.make_async_copy(wout_hbm, wout, load_sem.at[2])
-    load_feat.start()
-    load_win.start()
-    load_wout.start()
-    ag[NODE, own] = nodes[...]
-    ag[COT, own] = cot[...]
+    load_small = [
+        pltpu.make_async_copy(src_hbm, src.at[0], load_sem.at[0]),
+        pltpu.make_async_copy(tgt_hbm, tgt.at[0], load_sem.at[1]),
+    ]
+    for copy in load_small:
+        copy.start()
     barrier = pltpu.get_barrier_semaphore()
     peers = [sibling, across] + line
     for device in peers:
         pl.semaphore_signal(barrier, inc=1, device_id={"edge": device}, device_id_type=MESH)
+    ag[NODE, own] = nodes[...]
+    ag[COT, own] = cot[...]
     pl.semaphore_wait(barrier, len(peers))
-    ag_z(NODE)
+    for h in range(2):
+        ag_z(NODE, h)
+    for copy in load_small:
+        copy.wait()
 
     ids = src[...]
     owner = ids // rows
@@ -185,28 +197,20 @@
     hot[:, 0:total] = seen.T.astype(bf16)
     hot[:, total:total + 128] = near.T.astype(bf16)
 
-    load_feat.wait()
-    load_win.wait()
     tile = 256
     tiles = edges // tile
-
-    def first(t):
-        high, low = split(feat[t * tile:(t + 1) * tile])
-        wf = split(win[2 * width:3 * width])
-        pre[t * tile:(t + 1) * tile] = mm3((high, low), wf)
 
     def turn(t):
         high, low = split(feat[t * tile:(t + 1) * tile].T)
         eth[:, t * tile:(t + 1) * tile] = high
         etl[:, t * tile:(t + 1) * tile] = low
 
-    first(0)
-    ag_x(NODE)
+    for h in range(2):
+        ag_x(NODE, h)
     ag_z(COT)
-    first(1)
-    ag_c(NODE)
-    first(2)
-    load_wout.wait()
+    pre[...] = mm3(split(feat[...]), split(win[2 * width:3 * width]))
+    for h in range(2):
+        ag_c(NODE, h)
     zeros = jnp.zeros((128 - rows, width), bf16)
     th, tl = split(mm3(split(nodes[...]), split(win[width:2 * width])))
     tabh[total:total + 128] = jnp.concatenate([th, zeros], axis=0)
@@ -216,7 +220,8 @@
     bkl[...] = jnp.concatenate([tl, zeros], axis=0)
     for t in range(tiles):
         turn(t)
-    fin("ac", NODE)
+    for h in range(2):
+        fin("ac", NODE, h)
     th, tl = split(mm3(split(ag[NODE]), split(win[0:width])))
     tabh[0:total] = th
     tabl[0:total] = tl
@@ -241,19 +246,25 @@
     ag[HID, own] = g_sum
     ag_z(TGT)
     ag_z(HID)
-    part[0] = mm(hot_t[0:total], dh[...]) + mm(hot_t[0:total], dl[...])
-    rs_c(0)
+
+    def partial(j, side):
+        place = at(half, side * half)
+        if j == 0:
+            ones_t = hot_t[place]
+            part[j, place] = mm(ones_t, dh[...]) + mm(ones_t, dl[...])
+        else:
+            cut = at(half, (j - 1) * total + side * half)
+            part[j, place] = mm3((eth[cut], etl[cut]), (dh[...], dl[...]))
+
+    for j in range(3):
+        partial(j, 1 - c)
+        rs_c(j)
+    partial(0, c)
+    rs_x(0)
+    partial(1, c)
+    rs_x(1)
+    partial(2, c)
     ag_c(COT)
-
-    def outer(j):
-        cut = slice((j - 1) * total, j * total)
-        part[j] = mm3((eth[cut], etl[cut]), (dh[...], dl[...]))
-        rs_c(j)
-
-    outer(1)
-    rs_x(0)
-    outer(2)
-    rs_x(1)
     rs_z(0)
     rs_x(2)
     ag_x(TGT)
@@ -271,25 +282,34 @@
     rs_done(1, FA)
     ag_x(SRC)
     rs_done(2, FB)
-    fin("ac", TGT)
+    fin("ac", TGT, None)
     gin[width:2 * width] = mm3((ngth[...], ngtl[...]), split(ag[TGT])) * factor
     ag_x(FA)
     ag_c(SRC)
     ag_x(FB)
-    fin("ac", HID)
-    fin("ac", COT)
+    fin("ac", HID, None)
+    fin("ac", COT, None)
     gout[...] = mm3(split(ag[HID].T), split(ag[COT])) * factor
     ag_c(FA)
-    fin("ac", SRC)
+    fin("ac", SRC, None)
     gin[0:width] = mm3((ngth[...], ngtl[...]), split(ag[SRC])) * factor
     ag_c(FB)
-    fin("ac", FA)
+    fin("ac", FA, None)
     gin[2 * width:2 * width + total] = ag[FA] * factor
-    fin("ac", FB)
+    fin("ac", FB, None)
     gin[2 * width + total:3 * width] = ag[FB] * factor
     for copies in sent.values():
         for copy in copies:
             copy.wait_send()
+
+
+def write_out(*refs):
+    sem = refs[6]
+    copies = [pltpu.make_async_copy(refs[k], refs[3 + k], sem.at[k]) for k in range(3)]
+    for copy in copies:
+        copy.start()
+    for copy in copies:
+        copy.wait()
 
 
 def fused(n, nodes, edge_feat, source, target, w_in, w_out, cotangent):
@@ -302,32 +322,40 @@
     scratch = [
         ((7, total, width), f32), ((3, total, width), f32), ((3, total // 2, width), f32),
         ((3, total // 4, width), f32), ((3, zs - 1, rows, width), f32),
-        ((edges, width), f32), ((3 * width, width), f32), ((width, width), f32),
         ((width, edges), bf16), ((width, edges), bf16),
         ((total + 128, edges), bf16), ((edges, total + 128), bf16),
         ((total + 128, width), bf16), ((total + 128, width), bf16),
         ((128, width), bf16), ((128, width), bf16),
         ((edges, width), f32), ((edges, width), bf16), ((edges, width), bf16),
         ((width, total), bf16), ((width, total), bf16),
+        ((1, edges), jnp.int32), ((1, edges), jnp.int32),
     ]
-    copies = 10 * (zs + 1)
-    return pl.pallas_call(
+    copies = 11 * (zs + 1)
+    results = pl.pallas_call(
         functools.partial(kernel, n),
         out_shape=(
             jax.ShapeDtypeStruct((rows, width), f32),
             jax.ShapeDtypeStruct((3 * width, width), f32),
             jax.ShapeDtypeStruct((width, width), f32),
         ),
-        in_specs=[vmem] * 4 + [hbm] * 3,
+        in_specs=[vmem] * 2 + [hbm] * 2 + [vmem] * 3,
         out_specs=(vmem, vmem, vmem),
         scratch_shapes=[pltpu.VMEM(shape, kind) for shape, kind in scratch] + [
-            pltpu.SemaphoreType.DMA((3,)),
+            pltpu.SemaphoreType.DMA((2,)),
             pltpu.SemaphoreType.DMA((copies,)),
             pltpu.SemaphoreType.DMA((copies,)),
         ],
         compiler_params=pltpu.CompilerParams(
-            collective_id=0, has_side_effects=True, vmem_limit_bytes=52 * 2**20),
-    )(nodes, cotangent, source.reshape(1, edges), target.reshape(1, edges), edge_feat, w_in, w_out)
+            collective_id=0, has_side_effects=True, vmem_limit_bytes=32 * 2**20),
+    )(nodes, cotangent, source, target, edge_feat, w_in, w_out)
+    return pl.pallas_call(
+        write_out,
+        out_shape=tuple(jax.ShapeDtypeStruct(r.shape, r.dtype) for r in results),
+        in_specs=[hbm] * 3,
+        out_specs=(hbm,) * 3,
+        scratch_shapes=[pltpu.SemaphoreType.DMA((3,))],
+        compiler_params=pltpu.CompilerParams(vmem_limit_bytes=2 * 2**20),
+    )(*results)
 
 
 def body(nodes, edge_feat, source, target, w_in, w_out, cotangent):

time: 61.5 us -> 59.8 us (0.972)
  local copies, waits for them, and re-layouts: 8.34 us -> 7.4 us
  Pallas kernels: 52.2 us -> 51.3 us
    pallas_call x1, Pallas kernels: 52.2 us -> 49.2 us  [fused(): pl.pallas_call(functools.partial(kernel, n), out_shape=(jax.ShapeDtypeStr...]
    pallas_call x0 -> x1, Pallas kernels: none -> 2.04 us  [fused(): pl.pallas_call(write_out, out_shape=tuple((jax.ShapeDtypeStruct(r.shape,...]
    reshape x2 -> x0, local copies, waits for them, and re-layouts: 1.38 us -> none  [the longest x1 0.69 us: fused(): source.reshape(1, edges)]
    unnamed x7 -> x14, local copies, waits for them, and re-layouts: 6.96 us -> 7.4 us
where the time goes in v2:
time: 59.8 us; the launch traced here: 59.3 us
  Pallas kernels  51.3 us (86%)
  local copies, waits for them, and re-layouts  7.4 us (12%)
  between operations  0.66 us (1%)
    pallas_call x1, Pallas kernels, fused(): pl.pallas_call(functools.partial(kernel, n), out_shape=(jax.ShapeDtypeStr...  49.2 us
    unnamed x14, local copies, waits for them, and re-layouts  7.4 us
    pallas_call x1, Pallas kernels, fused(): pl.pallas_call(write_out, out_shape=tuple((jax.ShapeDtypeStruct(r.shape,...  2.04 us

profile of v2, /device:TPU:1, one launch (start us, length us, event | category | flops | bytes accessed | tf_op | source)
XLA Modules:
  0.0 59.3 jit_solution(6114996465946810758)
XLA Ops:
  0.6 0.0 copy-start
  0.6 1.9 %copy-done = f32[1536,512]{1,0:T(8,128)S(1)} copy-done((f32[1536,512]{1,0:T(8,128)S(1)}, f32[1536,512]{1,0:T(8,128)}, u32[]{:S(2)}) %copy-start) | copy-done | bytes 3145752
  2.5 0.0 copy-start.1
  2.5 1.4 %copy-done.1 = f32[768,512]{1,0:T(8,128)S(1)} copy-done((f32[768,512]{1,0:T(8,128)S(1)}, f32[768,512]{1,0:T(8,128)}, u32[]{:S(2)}) %copy-start.1) | copy-done | bytes 1572888
  3.9 0.0 copy-start.2
  3.9 1.2 %copy-done.2 = f32[512,512]{1,0:T(8,128)S(1)} copy-done((f32[512,512]{1,0:T(8,128)S(1)}, f32[512,512]{1,0:T(8,128)}, u32[]{:S(2)}) %copy-start.2) | copy-done | bytes 1048600
  5.2 0.0 copy-start.3
  5.2 0.8 %copy-done.3 = f32[16,512]{1,0:T(8,128)S(1)} copy-done((f32[16,512]{1,0:T(8,128)S(1)}, f32[16,512]{1,0:T(8,128)}, u32[]{:S(2)}) %copy-start.3) | copy-done | bytes 32792
  5.9 0.0 copy-start.4
  5.9 0.8 %copy-done.4 = f32[16,512]{1,0:T(8,128)S(1)} copy-done((f32[16,512]{1,0:T(8,128)S(1)}, f32[16,512]{1,0:T(8,128)}, u32[]{:S(2)}) %copy-start.4) | copy-done | bytes 32792
  6.7 0.0 copy-start.5
  6.7 0.7 %copy-done.5 = s32[768]{0:T(1024)S(1)} copy-done((s32[768]{0:T(1024)S(1)}, s32[768]{0:T(1024)}, u32[]{:S(2)}) %copy-start.5) | copy-done | bytes 3096
  7.4 0.0 copy-start.6
  7.4 0.7 %copy-done.6 = s32[768]{0:T(1024)S(1)} copy-done((s32[768]{0:T(1024)S(1)}, s32[768]{0:T(1024)}, u32[]{:S(2)}) %copy-start.6) | copy-done | bytes 3096
  8.0 49.2 %shard_map.94 = (f32[16,512]{1,0:T(8,128)S(1)}, f32[1536,512]{1,0:T(8,128)S(1)}, f32[512,512]{1,0:T(8,128)S(1)}) custom-call(f32[16,512]{1,0:T(8,128)S(1)} %copy-done.3, f32[16,512]{1,0:T(8,128)S(1)} %copy-done.4, s32[768]{0:T(1024)S(1)} %copy-done.5, s32[768]{0:T(1024)S(1)} %copy-done.6, f32[768,512]{1,0:T(8,128)S(1)} %copy-done.1, ...), custom_call_target="tpu_custom_call" | custom-call | tf_op jit(solution)/shard_map/pallas_call | solution.py:334
  57.3 2.0 %shard_map.95 = (f32[16,512]{1,0:T(8,128)}, f32[1536,512]{1,0:T(8,128)}, f32[512,512]{1,0:T(8,128)}) custom-call(f32[16,512]{1,0:T(8,128)S(1)} %get-tuple-element.6.refs_0_, f32[1536,512]{1,0:T(8,128)S(1)} %get-tuple-element.7.refs_1_, f32[512,512]{1,0:T(8,128)S(1)} %get-tuple-element.8.refs_2_), custom_call_target="tpu_custom_call" | custom-call | tf_op jit(solution)/shard_map/pallas_call | solution.py:351
Async XLA Ops:
  0.6 1.9 %copy-start = (f32[1536,512]{1,0:T(8,128)S(1)}, f32[1536,512]{1,0:T(8,128)}, u32[]{:S(2)}) copy-start(f32[1536,512]{1,0:T(8,128)} %win.1) | copy-start | bytes 9437188
  2.5 1.4 %copy-start.1 = (f32[768,512]{1,0:T(8,128)S(1)}, f32[768,512]{1,0:T(8,128)}, u32[]{:S(2)}) copy-start(f32[768,512]{1,0:T(8,128)} %feat.1) | copy-start | bytes 4718596
  3.9 1.2 %copy-start.2 = (f32[512,512]{1,0:T(8,128)S(1)}, f32[512,512]{1,0:T(8,128)}, u32[]{:S(2)}) copy-start(f32[512,512]{1,0:T(8,128)} %wout.1) | copy-start | bytes 3145732
  5.2 0.8 %copy-start.3 = (f32[16,512]{1,0:T(8,128)S(1)}, f32[16,512]{1,0:T(8,128)}, u32[]{:S(2)}) copy-start(f32[16,512]{1,0:T(8,128)} %nodes.1) | copy-start | bytes 98308
  5.9 0.8 %copy-start.4 = (f32[16,512]{1,0:T(8,128)S(1)}, f32[16,512]{1,0:T(8,128)}, u32[]{:S(2)}) copy-start(f32[16,512]{1,0:T(8,128)} %cot.1) | copy-start | bytes 98308
  6.7 0.7 %copy-start.5 = (s32[768]{0:T(1024)S(1)}, s32[768]{0:T(1024)}, u32[]{:S(2)}) copy-start(s32[768]{0:T(1024)} %src_hbm.1) | copy-start | bytes 9220
  7.4 0.7 %copy-start.6 = (s32[768]{0:T(1024)S(1)}, s32[768]{0:T(1024)}, u32[]{:S(2)}) copy-start(s32[768]{0:T(1024)} %tgt_hbm.1) | copy-start | bytes 9220

commit v3 on v2

--- a/solution.py
+++ b/solution.py
@@ -79,9 +79,9 @@
     return mm(ah, bh, dims) + (mm(ah, bl, dims) + mm(al, bh, dims))
 
 
-def kernel(n, nodes, cot, src_hbm, tgt_hbm, feat, win, wout, grads, gin, gout,
+def kernel(n, nodes_hbm, cot_hbm, src_hbm, tgt_hbm, feat_hbm, win_hbm, wout_hbm, grads, gin, gout,
            ag, part, rc, rx, rz, eth, etl, hot_t, hot,
-           tabh, tabl, bkh, bkl, pre, dh, dl, ngth, ngtl, src, tgt, load_sem, send_sem, recv_sem):
+           tabh, tabl, bkh, bkl, pre, dh, dl, ngth, ngtl, src, tgt, nodes, cot, feat, win, wout, load_sem, send_sem, recv_sem):
     f32, bf16 = jnp.float32, jnp.bfloat16
     rows, width = nodes.shape
     edges = src.shape[1]
@@ -171,12 +171,23 @@
         pltpu.make_async_copy(src_hbm, src.at[0], load_sem.at[0]),
         pltpu.make_async_copy(tgt_hbm, tgt.at[0], load_sem.at[1]),
     ]
-    for copy in load_small:
+    load_rows = [
+        pltpu.make_async_copy(nodes_hbm, nodes, load_sem.at[2]),
+        pltpu.make_async_copy(cot_hbm, cot, load_sem.at[3]),
+    ]
+    load_big = [
+        pltpu.make_async_copy(feat_hbm, feat, load_sem.at[4]),
+        pltpu.make_async_copy(win_hbm, win, load_sem.at[5]),
+        pltpu.make_async_copy(wout_hbm, wout, load_sem.at[6]),
+    ]
+    for copy in load_rows + load_small + load_big:
         copy.start()
     barrier = pltpu.get_barrier_semaphore()
     peers = [sibling, across] + line
     for device in peers:
         pl.semaphore_signal(barrier, inc=1, device_id={"edge": device}, device_id_type=MESH)
+    for copy in load_rows:
+        copy.wait()
     ag[NODE, own] = nodes[...]
     ag[COT, own] = cot[...]
     pl.semaphore_wait(barrier, len(peers))
@@ -208,6 +219,8 @@
     for h in range(2):
         ag_x(NODE, h)
     ag_z(COT)
+    for copy in load_big:
+        copy.wait()
     pre[...] = mm3(split(feat[...]), split(win[2 * width:3 * width]))
     for h in range(2):
         ag_c(NODE, h)
@@ -329,6 +342,8 @@
         ((edges, width), f32), ((edges, width), bf16), ((edges, width), bf16),
         ((width, total), bf16), ((width, total), bf16),
         ((1, edges), jnp.int32), ((1, edges), jnp.int32),
+        ((rows, width), f32), ((rows, width), f32),
+        ((edges, width), f32), ((3 * width, width), f32), ((width, width), f32),
     ]
     copies = 11 * (zs + 1)
     results = pl.pallas_call(
@@ -338,16 +353,17 @@
             jax.ShapeDtypeStruct((3 * width, width), f32),
             jax.ShapeDtypeStruct((width, width), f32),
         ),
-        in_specs=[vmem] * 2 + [hbm] * 2 + [vmem] * 3,
+        in_specs=[hbm] * 7,
         out_specs=(vmem, vmem, vmem),
         scratch_shapes=[pltpu.VMEM(shape, kind) for shape, kind in scratch] + [
-            pltpu.SemaphoreType.DMA((2,)),
+            pltpu.SemaphoreType.DMA((7,)),
             pltpu.SemaphoreType.DMA((copies,)),
             pltpu.SemaphoreType.DMA((copies,)),
         ],
         compiler_params=pltpu.CompilerParams(
             collective_id=0, has_side_effects=True, vmem_limit_bytes=32 * 2**20),
-    )(nodes, cotangent, source, target, edge_feat, w_in, w_out)
+    )(*[pltpu.with_memory_space_constraint(value, pltpu.HBM) for value in (
+        nodes, cotangent, source, target, edge_feat, w_in, w_out)])
     return pl.pallas_call(
         write_out,
         out_shape=tuple(jax.ShapeDtypeStruct(r.shape, r.dtype) for r in results),

time: 59.8 us -> 52.1 us (0.87)
  local copies, waits for them, and re-layouts: 7.4 us -> 0 us
    unnamed x14 -> x0, local copies, waits for them, and re-layouts: 7.4 us -> none
where the time goes in v3:
time: 52.1 us; the launch traced here: 52 us
  Pallas kernels  51.3 us (98%)
  between operations  0.64 us (1%)
    pallas_call x1, Pallas kernels, fused(): pl.pallas_call(functools.partial(kernel, n), out_shape=(jax.ShapeDtypeStr...  49.3 us
    pallas_call x1, Pallas kernels, fused(): pl.pallas_call(write_out, out_shape=tuple((jax.ShapeDtypeStruct(r.shape,...  2.04 us

profile of v3, /device:TPU:1, one launch (start us, length us, event | category | flops | bytes accessed | tf_op | source)
XLA Modules:
  0.0 52.0 jit_solution(2770028418137103677)
XLA Ops:
  0.6 49.3 %shard_map.94 = (f32[16,512]{1,0:T(8,128)S(1)}, f32[1536,512]{1,0:T(8,128)S(1)}, f32[512,512]{1,0:T(8,128)S(1)}) custom-call(f32[16,512]{1,0:T(8,128)} %nodes_hbm.1, f32[16,512]{1,0:T(8,128)} %cot_hbm.1, s32[768]{0:T(1024)} %src_hbm.1, s32[768]{0:T(1024)} %tgt_hbm.1, f32[768,512]{1,0:T(8,128)} %feat_hbm.1, f32[1536,512]{1,0:T(8,128)} %win_hbm.1, ...), custom_call_target="tpu_custom_call" | custom-call | tf_op jit(solution)/shard_map/pallas_call | solution.py:349
  49.9 2.0 %shard_map.95 = (f32[16,512]{1,0:T(8,128)}, f32[1536,512]{1,0:T(8,128)}, f32[512,512]{1,0:T(8,128)}) custom-call(f32[16,512]{1,0:T(8,128)S(1)} %get-tuple-element.6.refs_0_, f32[1536,512]{1,0:T(8,128)S(1)} %get-tuple-element.7.refs_1_, f32[512,512]{1,0:T(8,128)S(1)} %get-tuple-element.8.refs_2_), custom_call_target="tpu_custom_call" | custom-call | tf_op jit(solution)/shard_map/pallas_call | solution.py:367

commit v4 on v3

--- a/solution.py
+++ b/solution.py
@@ -159,13 +159,14 @@
             send(("rz", j), (7 + j) * per + 2 + k, part.at[j, at(rows, base + other * rows)],
                  rz.at[j, k], device)
 
-    def rs_done(j, i):
+    def rs_done(j, i, parts=(None,)):
         fin("rz", j)
         piece = part[j, own]
         for k in range(zs - 1):
             piece = piece + rz[j, k]
         ag[i, own] = piece
-        ag_z(i)
+        for h in parts:
+            ag_z(i, h)
 
     load_small = [
         pltpu.make_async_copy(src_hbm, src.at[0], load_sem.at[0]),
@@ -288,29 +289,32 @@
     rs_z(1)
     rs_done(0, SRC)
     rs_z(2)
+    rs_done(1, FA)
+    ag_x(SRC)
     ag_c(TGT)
+    rs_done(2, FB, (0, 1))
     ag_c(HID)
+    ag_x(FA)
+    fin("ac", TGT, None)
+    gin[width:2 * width] = mm3((ngth[...], ngtl[...]), split(ag[TGT])) * factor
+    ag_x(FB, 0)
+    ag_x(FB, 1)
+    ag_c(SRC)
     grads[...] = (mm3(split(ag[SRC, own]), split(win[0:width]), ((1,), (1,)))
                   + mm3(split(ag[TGT, own]), split(win[width:2 * width]), ((1,), (1,))))
-    rs_done(1, FA)
-    ag_x(SRC)
-    rs_done(2, FB)
-    fin("ac", TGT, None)
-    gin[width:2 * width] = mm3((ngth[...], ngtl[...]), split(ag[TGT])) * factor
-    ag_x(FA)
-    ag_c(SRC)
-    ag_x(FB)
     fin("ac", HID, None)
     fin("ac", COT, None)
     gout[...] = mm3(split(ag[HID].T), split(ag[COT])) * factor
     ag_c(FA)
     fin("ac", SRC, None)
     gin[0:width] = mm3((ngth[...], ngtl[...]), split(ag[SRC])) * factor
-    ag_c(FB)
+    ag_c(FB, 0)
     fin("ac", FA, None)
     gin[2 * width:2 * width + total] = ag[FA] * factor
-    fin("ac", FB, None)
-    gin[2 * width + total:3 * width] = ag[FB] * factor
+    ag_c(FB, 1)
+    for h in range(2):
+        fin("ac", FB, h)
+        gin[2 * width + total:3 * width, cols(h)] = ag[FB, :, cols(h)] * factor
     for copies in sent.values():
         for copy in copies:
             copy.wait_send()
@@ -345,7 +349,7 @@
         ((rows, width), f32), ((rows, width), f32),
         ((edges, width), f32), ((3 * width, width), f32), ((width, width), f32),
     ]
-    copies = 11 * (zs + 1)
+    copies = 17 * (zs + 1)
     results = pl.pallas_call(
         functools.partial(kernel, n),
         out_shape=(

time: 52.1 us -> 51.9 us (level)
  no operation moved by 1% of the time
where the time goes in v4:
time: 51.9 us; the launch traced here: 51.6 us
  Pallas kernels  51 us (98%)
  between operations  0.64 us (1%)
    pallas_call x1, Pallas kernels, fused(): pl.pallas_call(functools.partial(kernel, n), out_shape=(jax.ShapeDtypeStr...  48.9 us
    pallas_call x1, Pallas kernels, fused(): pl.pallas_call(write_out, out_shape=tuple((jax.ShapeDtypeStruct(r.shape,...  2.04 us

profile of v4, /device:TPU:1, one launch (start us, length us, event | category | flops | bytes accessed | tf_op | source)
XLA Modules:
  0.0 51.6 jit_solution(6220125963820443471)
XLA Ops:
  0.6 48.9 %shard_map.94 = (f32[16,512]{1,0:T(8,128)S(1)}, f32[1536,512]{1,0:T(8,128)S(1)}, f32[512,512]{1,0:T(8,128)S(1)}) custom-call(f32[16,512]{1,0:T(8,128)} %nodes_hbm.1, f32[16,512]{1,0:T(8,128)} %cot_hbm.1, s32[768]{0:T(1024)} %src_hbm.1, s32[768]{0:T(1024)} %tgt_hbm.1, f32[768,512]{1,0:T(8,128)} %feat_hbm.1, f32[1536,512]{1,0:T(8,128)} %win_hbm.1, ...), custom_call_target="tpu_custom_call" | custom-call | tf_op jit(solution)/shard_map/pallas_call | solution.py:353
  49.6 2.0 %shard_map.95 = (f32[16,512]{1,0:T(8,128)}, f32[1536,512]{1,0:T(8,128)}, f32[512,512]{1,0:T(8,128)}) custom-call(f32[16,512]{1,0:T(8,128)S(1)} %get-tuple-element.6.refs_0_, f32[1536,512]{1,0:T(8,128)S(1)} %get-tuple-element.7.refs_1_, f32[512,512]{1,0:T(8,128)S(1)} %get-tuple-element.8.refs_2_), custom_call_target="tpu_custom_call" | custom-call | tf_op jit(solution)/shard_map/pallas_call | solution.py:371
